TPU v7x, 128 devices: a whole 4x4x4 slice. The times are simulated.
128 devices in a mesh: row: 8 (over y_hi, z), col: 16 (over y_lo, x, core).
Axes of the slice: x: 4, y: 4 (y_hi: 2, y_lo: 2; y = y_hi * 2 + y_lo), z: 4, core: 2. Of those that a mesh axis runs over, the one named last changes fastest.
Arguments:
- vectors: bfloat16 [65536, 256], P(('row', 'col')), may hold values from -6 to 6
- blocks: bfloat16 [8, 16, 256, 128, 128], P('row', 'col'), may hold values from -0.046875 to 0.046875
- block_rows: int32 [8, 16, 256], P('row', 'col'), may hold values from 0 to 63
- block_cols: int32 [8, 16, 256], P('row', 'col'), may hold values from 0 to 31
- block_count: int32 [8, 16], P('row', 'col'), may hold values from 32 to 256, as said below
- lower_edge: float32 [1], replicated, may hold values from -0.6 to -0.3
- upper_edge: float32 [1], replicated, may hold values from 1 to 2
Outputs:
- filtered: float32 [65536, 256], P(('row', 'col'))
Inputs may be any that keep to these rules, and one draw needn't show every extreme that they name: `block_count`: some device has all 256 slots live.
All inputs are finite; a program needn't handle non-finite values.
Results may differ from a plain program's by a relative error of at most 0.008.
Values may be sent and summed in bfloat16 or wider, within the bound.
No kernel may reach another device: no remote copies, remote signals or barrier semaphores. Data moves between devices by JAX's collectives and lax.ppermute only.
A program may use at most 192 MiB of HBM per device.

v0:
```python
import jax
import jax.numpy as jnp
from jax import lax
from jax.sharding import PartitionSpec as P

DEGREE = 2


def pick_table(indices, count):
    return (indices[:, None] == jnp.arange(count, dtype=jnp.int32)[None, :]).astype(jnp.bfloat16)


def place_sum(table, values):
    upper = values.astype(jnp.bfloat16)
    lower = (values - upper.astype(jnp.float32)).astype(jnp.bfloat16)
    first = jnp.einsum("gt,giv->tiv", table, upper, preferred_element_type=jnp.float32)
    second = jnp.einsum("gt,giv->tiv", table, lower, preferred_element_type=jnp.float32)
    return first + second


def slot_products(
    local_blocks, local_rows, local_cols, slot_count, rows_side, cols_side, group_size, group_limit
):
    block_size = local_blocks.shape[1]
    vec_width = rows_side.shape[1]
    row_tiles = rows_side.reshape(-1, block_size, vec_width)
    col_tiles = cols_side.reshape(-1, block_size, vec_width)
    row_count = row_tiles.shape[0]
    col_count = col_tiles.shape[0]

    def group_step(position, totals):
        row_totals, col_totals = totals
        first_slot = position * group_size
        block_tile = lax.dynamic_slice_in_dim(local_blocks, first_slot, group_size, 0)
        rows_here = lax.dynamic_slice_in_dim(local_rows, first_slot, group_size, 0)
        cols_here = lax.dynamic_slice_in_dim(local_cols, first_slot, group_size, 0)
        live_mask = (first_slot + jnp.arange(group_size) < slot_count).astype(jnp.float32)[
            :, None, None
        ]
        row_table = pick_table(rows_here, row_count)
        col_table = pick_table(cols_here, col_count)
        col_picked = jnp.einsum(
            "gt,tjv->gjv", col_table, col_tiles, preferred_element_type=jnp.float32
        ).astype(jnp.bfloat16)
        row_picked = jnp.einsum(
            "gt,tjv->gjv", row_table, row_tiles, preferred_element_type=jnp.float32
        ).astype(jnp.bfloat16)
        forward = (
            jnp.einsum("gij,gjv->giv", block_tile, col_picked, preferred_element_type=jnp.float32)
            * live_mask
        )
        mirror = (
            jnp.einsum("gji,gjv->giv", block_tile, row_picked, preferred_element_type=jnp.float32)
            * live_mask
        )
        return (
            row_totals + place_sum(row_table, forward),
            col_totals + place_sum(col_table, mirror),
        )

    start_totals = (
        jnp.zeros(row_tiles.shape, jnp.float32),
        jnp.zeros(col_tiles.shape, jnp.float32),
    )
    row_totals, col_totals = lax.fori_loop(0, group_limit, group_step, start_totals)
    return (row_totals.reshape(-1, vec_width), col_totals.reshape(-1, vec_width))


def per_device(vectors, blocks, block_rows, block_cols, block_count, lower_edge, upper_edge):
    center = (upper_edge[0] + lower_edge[0]) * 0.5
    half_width = (upper_edge[0] - lower_edge[0]) * 0.5
    local_blocks = blocks[0, 0]
    local_rows = block_rows[0, 0]
    local_cols = block_cols[0, 0]
    slot_count = block_count[0, 0]
    group_size = min(64, local_blocks.shape[0])
    group_limit = local_blocks.shape[0] // group_size
    current = vectors.astype(jnp.float32)
    previous = jnp.zeros_like(current)
    for degree in range(DEGREE):
        operand = current.astype(jnp.bfloat16)
        cols_side = lax.all_gather(operand, "row", axis=0, tiled=True)
        rows_side = lax.all_gather(operand, "col", axis=0, tiled=True)
        row_part, col_part = slot_products(
            local_blocks,
            local_rows,
            local_cols,
            slot_count,
            rows_side,
            cols_side,
            group_size,
            group_limit,
        )
        forward = lax.psum_scatter(row_part, "col", scatter_dimension=0, tiled=True)
        applied = forward + lax.psum_scatter(col_part, "row", scatter_dimension=0, tiled=True)
        shifted = applied - center * current
        if degree == 0:
            following = shifted / half_width
        else:
            following = 2.0 * shifted / half_width - previous
        previous, current = (current, following)
    return current


def solution(mesh):
    return jax.shard_map(
        per_device,
        mesh=mesh,
        in_specs=(
            P(("row", "col"), None),
            P("row", "col", None, None, None),
            P("row", "col", None),
            P("row", "col", None),
            P("row", "col"),
            P(),
            P(),
        ),
        out_specs=P(("row", "col"), None),
        check_vma=False,
    )
```

profile of v0, /device:TPU:1, one launch (start us, length us, event | category | flops | bytes accessed | tf_op | source)
XLA Modules:
  0.0 994.5 jit_solution(9181128054311836283)
XLA Ops:
  8.1 58.6 %all-gather.5.cloned.1.call-done = bf16[4096,256]{1,0:T(8,128)(2,1)} async-done(((bf16[512,256]{1,0:T(8,128)(2,1)}), bf16[4096,256]{1,0:T(8,128)(2,1)}) %all-gather.5.cloned.1.call-update) | async-done | bytes 2097168 | tf_op jit(solution)/shard_map/all_gather | solution.py:82
  66.7 37.6 %all-gather.7.cloned.1.call-done = bf16[8192,256]{1,0:T(8,128)(2,1)} async-done(((bf16[512,256]{1,0:T(8,128)(2,1)}), bf16[8192,256]{1,0:T(8,128)(2,1)}) %all-gather.7.cloned.1.call-update) | async-done | bytes 4194320 | tf_op jit(solution)/shard_map/all_gather | solution.py:83
  104.3 230.7 %while.32 = (s32[]{:T(128)}, f32[64,128,256]{2,0,1:T(8,128)}, f32[32,128,256]{2,0,1:T(8,128)}, s32[256]{0:T(256)}, bf16[256,128,128]{2,1,0:T(8,128)(2,1)}, /*ind...) while((s32[]{:T(128)}, f32[64,128,256]{2,0,1:T(8,128)}, ...), condition=%wide.region_1.0_spmd.clone, body=%wide.region_0.0_spmd.clone.sunk | while | flops 2312128768 | bytes 178265392 | solution.py:65
  108.2 8.0 fusion.125
  116.3 3.3 fusion.126
  120.2 13.1 %multiply_convert_fusion.6 = (bf16[64,128,256]{2,1,0:T(8,128)(2,1)}, bf16[64,128,256]{2,1,0:T(8,128)(2,1)}, bf16[64,128,256]{2,1,0:T(8,128)(2,1)}, bf16[64,128,256]{2,1,0:T(8,128)(2,1)}) fusion(f32[64]{0:T(128)S(1)} %compare_convert_fusion.4, f32[64,128,256]{2,1,0:T(8,128)} %fusion.125, bf16[64,128,256]{2,0,1:T(8,128)(2,1)S(1)} %fusion.126, ...), kind=kOutput, calls=%fused_computation.5.clone.2 | convolution fusion | flops 557842432 | bytes 31457540 | tf_op jit(solution)/shard_map/while/body/eval_jaxpr/gji,gjv->giv/dot_general | solution.py:53
  133.3 7.2 fusion.128
  140.4 9.0 select_add_fusion.9
  149.4 3.3 fusion.127
  152.7 6.7 select_add_fusion.8
  163.2 8.0 fusion.125
  175.3 13.1 %multiply_convert_fusion.6 = (bf16[64,128,256]{2,1,0:T(8,128)(2,1)}, bf16[64,128,256]{2,1,0:T(8,128)(2,1)}, bf16[64,128,256]{2,1,0:T(8,128)(2,1)}, bf16[64,128,256]{2,1,0:T(8,128)(2,1)}) fusion(f32[64]{0:T(128)S(1)} %compare_convert_fusion.4, f32[64,128,256]{2,1,0:T(8,128)} %fusion.125, bf16[64,128,256]{2,0,1:T(8,128)(2,1)S(1)} %fusion.126, ...), kind=kOutput, calls=%fused_computation.5.clone.2 | convolution fusion | flops 557842432 | bytes 31457540 | tf_op jit(solution)/shard_map/while/body/eval_jaxpr/gji,gjv->giv/dot_general | solution.py:53
  188.3 7.2 fusion.128
  195.5 10.2 %select_add_fusion.9 = f32[32,128,256]{2,0,1:T(8,128)} fusion(f32[32,128,256]{2,0,1:T(8,128)} %get-tuple-element.568, f32[32,128,256]{2,0,1:T(8,128)} %fusion.128, bf16[64,128,256]{2,1,0:T(8,128)(2,1)} %get-tuple-element.539, pred[]{:T(512)S(6)} %compare.6, s32[64]{0:T(128)S(1)} %dynamic_slice.70), kind=kOutput, calls=%fused_computation.19.clone.1 | convolution fusion | flops 137365504 | bytes 16777472 | tf_op jit(solution)/shard_map/while/body/eval_jaxpr/gt,giv->tiv/dot_general | solution.py:16
  205.7 3.3 fusion.127
  209.0 8.8 select_add_fusion.8
  221.7 8.0 fusion.125
  229.7 3.3 fusion.126
  233.7 13.1 %multiply_convert_fusion.6 = (bf16[64,128,256]{2,1,0:T(8,128)(2,1)}, bf16[64,128,256]{2,1,0:T(8,128)(2,1)}, bf16[64,128,256]{2,1,0:T(8,128)(2,1)}, bf16[64,128,256]{2,1,0:T(8,128)(2,1)}) fusion(f32[64]{0:T(128)S(1)} %compare_convert_fusion.4, f32[64,128,256]{2,1,0:T(8,128)} %fusion.125, bf16[64,128,256]{2,0,1:T(8,128)(2,1)S(1)} %fusion.126, ...), kind=kOutput, calls=%fused_computation.5.clone.2 | convolution fusion | flops 557842432 | bytes 31457540 | tf_op jit(solution)/shard_map/while/body/eval_jaxpr/gji,gjv->giv/dot_general | solution.py:53
  246.7 7.2 fusion.128
  253.9 10.2 %select_add_fusion.9 = f32[32,128,256]{2,0,1:T(8,128)} fusion(f32[32,128,256]{2,0,1:T(8,128)} %get-tuple-element.568, f32[32,128,256]{2,0,1:T(8,128)} %fusion.128, bf16[64,128,256]{2,1,0:T(8,128)(2,1)} %get-tuple-element.539, pred[]{:T(512)S(6)} %compare.6, s32[64]{0:T(128)S(1)} %dynamic_slice.70), kind=kOutput, calls=%fused_computation.19.clone.1 | convolution fusion | flops 137365504 | bytes 16777472 | tf_op jit(solution)/shard_map/while/body/eval_jaxpr/gt,giv->tiv/dot_general | solution.py:16
  264.1 3.3 fusion.127
  267.4 8.8 select_add_fusion.8
  280.1 8.0 fusion.125
  292.1 13.1 %multiply_convert_fusion.6 = (bf16[64,128,256]{2,1,0:T(8,128)(2,1)}, bf16[64,128,256]{2,1,0:T(8,128)(2,1)}, bf16[64,128,256]{2,1,0:T(8,128)(2,1)}, bf16[64,128,256]{2,1,0:T(8,128)(2,1)}) fusion(f32[64]{0:T(128)S(1)} %compare_convert_fusion.4, f32[64,128,256]{2,1,0:T(8,128)} %fusion.125, bf16[64,128,256]{2,0,1:T(8,128)(2,1)S(1)} %fusion.126, ...), kind=kOutput, calls=%fused_computation.5.clone.2 | convolution fusion | flops 557842432 | bytes 31457540 | tf_op jit(solution)/shard_map/while/body/eval_jaxpr/gji,gjv->giv/dot_general | solution.py:53
  305.2 7.2 fusion.128
  312.4 10.2 %select_add_fusion.9 = f32[32,128,256]{2,0,1:T(8,128)} fusion(f32[32,128,256]{2,0,1:T(8,128)} %get-tuple-element.568, f32[32,128,256]{2,0,1:T(8,128)} %fusion.128, bf16[64,128,256]{2,1,0:T(8,128)(2,1)} %get-tuple-element.539, pred[]{:T(512)S(6)} %compare.6, s32[64]{0:T(128)S(1)} %dynamic_slice.70), kind=kOutput, calls=%fused_computation.19.clone.1 | convolution fusion | flops 137365504 | bytes 16777472 | tf_op jit(solution)/shard_map/while/body/eval_jaxpr/gt,giv->tiv/dot_general | solution.py:16
  322.5 3.3 fusion.127
  325.8 8.8 select_add_fusion.8
  335.0 6.6 copy.19
  341.6 11.5 %copy.18 = f32[64,128,256]{2,1,0:T(8,128)} copy(f32[64,128,256]{2,0,1:T(8,128)} %get-tuple-element.315) | data formatting | bytes 16777216 | tf_op jit(solution)/shard_map/while | solution.py:65
  354.5 70.5 %reduce-scatter.7.cloned.1.call-done = f32[512,256]{1,0:T(8,128)} async-done(((f32[4096,256]{1,0:T(8,128)}), f32[512,256]{1,0:T(8,128)}) %reduce-scatter.7.cloned.1.call-update) | async-done | bytes 524304 | tf_op jit(solution)/shard_map/reduce_scatter | solution.py:95
  425.1 72.9 %reduce-scatter.5.cloned.1.call-done = f32[512,256]{1,0:T(8,128)} async-done(((f32[8192,256]{1,0:T(8,128)}), f32[512,256]{1,0:T(8,128)}) %reduce-scatter.5.cloned.1.call-update) | async-done | bytes 524304 | tf_op jit(solution)/shard_map/reduce_scatter | solution.py:94
  500.7 56.0 %all-gather.9.cloned.1.call-done = bf16[4096,256]{1,0:T(8,128)(2,1)} async-done(((bf16[512,256]{1,0:T(8,128)(2,1)}), bf16[4096,256]{1,0:T(8,128)(2,1)}) %all-gather.9.cloned.1.call-update) | async-done | bytes 2097168 | tf_op jit(solution)/shard_map/all_gather | solution.py:82
  556.7 37.5 %all-gather.11.cloned.1.call-done = bf16[8192,256]{1,0:T(8,128)(2,1)} async-done(((bf16[512,256]{1,0:T(8,128)(2,1)}), bf16[8192,256]{1,0:T(8,128)(2,1)}) %all-gather.11.cloned.1.call-update) | async-done | bytes 4194320 | tf_op jit(solution)/shard_map/all_gather | solution.py:83
  594.2 227.8 %while.33 = (s32[]{:T(128)}, f32[64,128,256]{2,0,1:T(8,128)}, f32[32,128,256]{2,0,1:T(8,128)}, s32[256]{0:T(256)S(1)}, bf16[256,128,128]{2,1,0:T(8,128)(2,1)}, /...) while((s32[]{:T(128)}, f32[64,128,256]{2,0,1:T(8,128)}, ...), condition=%wide.region_5.0_spmd.clone, body=%wide.region_4.0_spmd.clone.sunk | while | flops 2312128768 | bytes 178261264 | solution.py:65
  597.6 8.0 fusion.143
  609.6 13.1 %multiply_convert_fusion.7 = (bf16[64,128,256]{2,1,0:T(8,128)(2,1)}, bf16[64,128,256]{2,1,0:T(8,128)(2,1)}, bf16[64,128,256]{2,1,0:T(8,128)(2,1)}, bf16[64,128,256]{2,1,0:T(8,128)(2,1)}) fusion(f32[64]{0:T(128)S(1)} %compare_convert_fusion.5, f32[64,128,256]{2,1,0:T(8,128)} %fusion.143, bf16[64,128,256]{2,0,1:T(8,128)(2,1)S(1)} %fusion.144, ...), kind=kOutput, calls=%fused_computation.42.clone.2 | convolution fusion | flops 557842432 | bytes 31457540 | tf_op jit(solution)/shard_map/while/body/eval_jaxpr/gji,gjv->giv/dot_general | solution.py:53
  622.6 7.2 fusion.146
  629.8 9.0 select_add_fusion.11
  638.8 3.3 fusion.145
  642.1 6.7 select_add_fusion.10
  651.9 8.0 fusion.143
  663.9 13.1 %multiply_convert_fusion.7 = (bf16[64,128,256]{2,1,0:T(8,128)(2,1)}, bf16[64,128,256]{2,1,0:T(8,128)(2,1)}, bf16[64,128,256]{2,1,0:T(8,128)(2,1)}, bf16[64,128,256]{2,1,0:T(8,128)(2,1)}) fusion(f32[64]{0:T(128)S(1)} %compare_convert_fusion.5, f32[64,128,256]{2,1,0:T(8,128)} %fusion.143, bf16[64,128,256]{2,0,1:T(8,128)(2,1)S(1)} %fusion.144, ...), kind=kOutput, calls=%fused_computation.42.clone.2 | convolution fusion | flops 557842432 | bytes 31457540 | tf_op jit(solution)/shard_map/while/body/eval_jaxpr/gji,gjv->giv/dot_general | solution.py:53
  677.0 7.2 fusion.146
  684.2 10.2 %select_add_fusion.11 = f32[32,128,256]{2,0,1:T(8,128)} fusion(f32[32,128,256]{2,0,1:T(8,128)} %get-tuple-element.607, f32[32,128,256]{2,0,1:T(8,128)} %fusion.146, bf16[64,128,256]{2,1,0:T(8,128)(2,1)} %get-tuple-element.552, pred[]{:T(512)S(6)} %compare.7, s32[64]{0:T(128)S(1)} %dynamic_slice.74), kind=kOutput, calls=%fused_computation.56.clone.1 | convolution fusion | flops 137365504 | bytes 16777472 | tf_op jit(solution)/shard_map/while/body/eval_jaxpr/gt,giv->tiv/dot_general | solution.py:16
  694.3 3.3 fusion.145
  697.6 8.8 select_add_fusion.10
  709.6 8.0 fusion.143
  721.6 13.1 %multiply_convert_fusion.7 = (bf16[64,128,256]{2,1,0:T(8,128)(2,1)}, bf16[64,128,256]{2,1,0:T(8,128)(2,1)}, bf16[64,128,256]{2,1,0:T(8,128)(2,1)}, bf16[64,128,256]{2,1,0:T(8,128)(2,1)}) fusion(f32[64]{0:T(128)S(1)} %compare_convert_fusion.5, f32[64,128,256]{2,1,0:T(8,128)} %fusion.143, bf16[64,128,256]{2,0,1:T(8,128)(2,1)S(1)} %fusion.144, ...), kind=kOutput, calls=%fused_computation.42.clone.2 | convolution fusion | flops 557842432 | bytes 31457540 | tf_op jit(solution)/shard_map/while/body/eval_jaxpr/gji,gjv->giv/dot_general | solution.py:53
  734.7 7.2 fusion.146
  741.9 10.2 %select_add_fusion.11 = f32[32,128,256]{2,0,1:T(8,128)} fusion(f32[32,128,256]{2,0,1:T(8,128)} %get-tuple-element.607, f32[32,128,256]{2,0,1:T(8,128)} %fusion.146, bf16[64,128,256]{2,1,0:T(8,128)(2,1)} %get-tuple-element.552, pred[]{:T(512)S(6)} %compare.7, s32[64]{0:T(128)S(1)} %dynamic_slice.74), kind=kOutput, calls=%fused_computation.56.clone.1 | convolution fusion | flops 137365504 | bytes 16777472 | tf_op jit(solution)/shard_map/while/body/eval_jaxpr/gt,giv->tiv/dot_general | solution.py:16
  752.0 3.3 fusion.145
  755.3 8.8 select_add_fusion.10
  767.3 8.0 fusion.143
  779.3 13.1 %multiply_convert_fusion.7 = (bf16[64,128,256]{2,1,0:T(8,128)(2,1)}, bf16[64,128,256]{2,1,0:T(8,128)(2,1)}, bf16[64,128,256]{2,1,0:T(8,128)(2,1)}, bf16[64,128,256]{2,1,0:T(8,128)(2,1)}) fusion(f32[64]{0:T(128)S(1)} %compare_convert_fusion.5, f32[64,128,256]{2,1,0:T(8,128)} %fusion.143, bf16[64,128,256]{2,0,1:T(8,128)(2,1)S(1)} %fusion.144, ...), kind=kOutput, calls=%fused_computation.42.clone.2 | convolution fusion | flops 557842432 | bytes 31457540 | tf_op jit(solution)/shard_map/while/body/eval_jaxpr/gji,gjv->giv/dot_general | solution.py:53
  792.4 7.2 fusion.146
  799.6 10.2 %select_add_fusion.11 = f32[32,128,256]{2,0,1:T(8,128)} fusion(f32[32,128,256]{2,0,1:T(8,128)} %get-tuple-element.607, f32[32,128,256]{2,0,1:T(8,128)} %fusion.146, bf16[64,128,256]{2,1,0:T(8,128)(2,1)} %get-tuple-element.552, pred[]{:T(512)S(6)} %compare.7, s32[64]{0:T(128)S(1)} %dynamic_slice.74), kind=kOutput, calls=%fused_computation.56.clone.1 | convolution fusion | flops 137365504 | bytes 16777472 | tf_op jit(solution)/shard_map/while/body/eval_jaxpr/gt,giv->tiv/dot_general | solution.py:16
  809.7 3.3 fusion.145
  813.0 8.8 select_add_fusion.10
  822.1 6.6 copy.21
  828.7 11.5 %copy.20 = f32[64,128,256]{2,1,0:T(8,128)} copy(f32[64,128,256]{2,0,1:T(8,128)} %get-tuple-element.317) | data formatting | bytes 16777216 | tf_op jit(solution)/shard_map/while | solution.py:65
  840.2 72.0 %reduce-scatter.11.cloned.1.call-done = f32[512,256]{1,0:T(8,128)} async-done(((f32[4096,256]{1,0:T(8,128)}), f32[512,256]{1,0:T(8,128)}) %reduce-scatter.11.cloned.1.call-update) | async-done | bytes 524304 | tf_op jit(solution)/shard_map/reduce_scatter | solution.py:95
  912.2 72.9 %reduce-scatter.9.cloned.1.call-done = f32[512,256]{1,0:T(8,128)} async-done(((f32[8192,256]{1,0:T(8,128)}), f32[512,256]{1,0:T(8,128)}) %reduce-scatter.9.cloned.1.call-update) | async-done | bytes 524304 | tf_op jit(solution)/shard_map/reduce_scatter | solution.py:94
  (128 shorter events, 60.1 us)
Async XLA Ops:
  6.5 60.2 %all-gather.5.cloned.1.call-start = ((), (), s32[]{:S(2)}) async-start(), calls=%async_computation.4 | async-start | bytes 2359296 | tf_op jit(solution)/shard_map/all_gather | solution.py:82
  7.3 97.0 %all-gather.7.cloned.1.call-start = ((), (), s32[]{:S(2)}) async-start(), calls=%async_computation.5 | async-start | bytes 4456448 | tf_op jit(solution)/shard_map/all_gather | solution.py:83
  8.0 417.1 %reduce-scatter.7.cloned.1.call-start = ((), (), s32[]{:S(2)}) async-start(), calls=%async_computation.7 | async-start | bytes 4718592 | tf_op jit(solution)/shard_map/reduce_scatter | solution.py:95
  108.1 8.0 copy-start.10
  108.2 8.1 copy-start.5
  140.4 9.0 copy-start
  149.4 3.3 copy-start.2
  163.2 8.0 copy-start.10
  163.2 8.1 copy-start.5
  195.5 10.2 %copy-start = (bf16[64,128,256]{2,1,0:T(8,128)(2,1)S(1)}, bf16[64,128,256]{2,1,0:T(8,128)(2,1)}, u32[]{:S(2)}) copy-start(bf16[64,128,256]{2,1,0:T(8,128)(2,1)} %get-tuple-element.536) | copy-start | bytes 12582916 | tf_op jit(solution)/shard_map/while
  205.7 3.3 copy-start.2
  221.6 8.0 copy-start.10
  221.6 8.1 copy-start.5
  253.9 10.2 %copy-start = (bf16[64,128,256]{2,1,0:T(8,128)(2,1)S(1)}, bf16[64,128,256]{2,1,0:T(8,128)(2,1)}, u32[]{:S(2)}) copy-start(bf16[64,128,256]{2,1,0:T(8,128)(2,1)} %get-tuple-element.536) | copy-start | bytes 12582916 | tf_op jit(solution)/shard_map/while
  264.1 3.3 copy-start.2
  280.0 8.0 copy-start.10
  280.1 8.1 copy-start.5
  312.4 10.2 %copy-start = (bf16[64,128,256]{2,1,0:T(8,128)(2,1)S(1)}, bf16[64,128,256]{2,1,0:T(8,128)(2,1)}, u32[]{:S(2)}) copy-start(bf16[64,128,256]{2,1,0:T(8,128)(2,1)} %get-tuple-element.536) | copy-start | bytes 12582916 | tf_op jit(solution)/shard_map/while
  322.5 3.3 copy-start.2
  341.6 156.4 %reduce-scatter.5.cloned.1.call-start = ((), (), s32[]{:S(2)}) async-start(), calls=%async_computation.6 | async-start | bytes 8912896 | tf_op jit(solution)/shard_map/reduce_scatter | solution.py:94
  353.1 144.9 %copy-start.6 = (bf16[512,256]{1,0:T(8,128)(2,1)S(1)}, bf16[512,256]{1,0:T(8,128)(2,1)}, u32[]{:S(2)}) copy-start(bf16[512,256]{1,0:T(8,128)(2,1)} %param.11) | copy-start | bytes 786436
  353.1 241.1 %copy-start.11 = (s32[256]{0:T(256)S(1)}, s32[256]{0:T(256)}, u32[]{:S(2)}) copy-start(s32[256]{0:T(256)} %get-tuple-element.664) | copy-start | bytes 3076
  353.1 241.1 %copy-start.12 = (s32[256]{0:T(256)S(1)}, s32[256]{0:T(256)}, u32[]{:S(2)}) copy-start(s32[256]{0:T(256)} %get-tuple-element.665) | copy-start | bytes 3076
  353.2 203.5 %all-gather.9.cloned.1.call-start = ((), (), s32[]{:S(2)}) async-start(), calls=%async_computation.8 | async-start | bytes 2359296 | tf_op jit(solution)/shard_map/all_gather | solution.py:82
  500.0 94.2 %all-gather.11.cloned.1.call-start = ((), (), s32[]{:S(2)}) async-start(), calls=%async_computation.9 | async-start | bytes 4456448 | tf_op jit(solution)/shard_map/all_gather | solution.py:83
  500.6 411.6 %reduce-scatter.11.cloned.1.call-start = ((), (), s32[]{:S(2)}) async-start(), calls=%async_computation.11 | async-start | bytes 4718592 | tf_op jit(solution)/shard_map/reduce_scatter | solution.py:95
  597.6 8.0 copy-start.4
  629.8 9.0 copy-start.1
  638.8 3.3 copy-start.3
  651.9 8.0 copy-start.4
  684.2 10.2 %copy-start.1 = (bf16[64,128,256]{2,1,0:T(8,128)(2,1)S(1)}, bf16[64,128,256]{2,1,0:T(8,128)(2,1)}, u32[]{:S(2)}) copy-start(bf16[64,128,256]{2,1,0:T(8,128)(2,1)} %get-tuple-element.549) | copy-start | bytes 12582916 | tf_op jit(solution)/shard_map/while
  694.3 3.3 copy-start.3
  709.6 8.0 copy-start.4
  741.9 10.2 %copy-start.1 = (bf16[64,128,256]{2,1,0:T(8,128)(2,1)S(1)}, bf16[64,128,256]{2,1,0:T(8,128)(2,1)}, u32[]{:S(2)}) copy-start(bf16[64,128,256]{2,1,0:T(8,128)(2,1)} %get-tuple-element.549) | copy-start | bytes 12582916 | tf_op jit(solution)/shard_map/while
  752.0 3.3 copy-start.3
  767.3 8.0 copy-start.4
  799.6 10.2 %copy-start.1 = (bf16[64,128,256]{2,1,0:T(8,128)(2,1)S(1)}, bf16[64,128,256]{2,1,0:T(8,128)(2,1)}, u32[]{:S(2)}) copy-start(bf16[64,128,256]{2,1,0:T(8,128)(2,1)} %get-tuple-element.549) | copy-start | bytes 12582916 | tf_op jit(solution)/shard_map/while
  809.7 3.3 copy-start.3
  828.7 156.5 %reduce-scatter.9.cloned.1.call-start = ((), (), s32[]{:S(2)}) async-start(), calls=%async_computation.10 | async-start | bytes 8912896 | tf_op jit(solution)/shard_map/reduce_scatter | solution.py:94
  840.2 144.9 %copy-start.7 = (bf16[512,256]{1,0:T(8,128)(2,1)S(1)}, bf16[512,256]{1,0:T(8,128)(2,1)}, u32[]{:S(2)}) copy-start(bf16[512,256]{1,0:T(8,128)(2,1)} %param.11) | copy-start | bytes 786436
  840.2 144.9 %copy-start.8 = (f32[512,256]{1,0:T(8,128)S(1)}, f32[512,256]{1,0:T(8,128)}, u32[]{:S(2)}) copy-start(f32[512,256]{1,0:T(8,128)} %reduce-scatter.7.cloned.1.call-done) | copy-start | bytes 1572868
  840.2 144.9 %copy-start.9 = (f32[512,256]{1,0:T(8,128)S(1)}, f32[512,256]{1,0:T(8,128)}, u32[]{:S(2)}) copy-start(f32[512,256]{1,0:T(8,128)} %reduce-scatter.5.cloned.1.call-done) | copy-start | bytes 1572868
Sparse Core Ops, SparseCore 0:
  9.7 56.9 all-gather.4
  68.4 35.8 all-gather.6
  341.7 83.3 reduce-scatter.6
  427.5 70.4 reduce-scatter.4
  500.5 56.1 all-gather.8
  558.4 35.8 all-gather.10
  828.8 83.3 reduce-scatter.10
  914.6 70.4 reduce-scatter.8
where the time goes:
time: 1010 us; the launch traced here: 995 us
  waiting for transfers between devices  480 us (48%)
  matrix products  448 us (44%)
  local copies, waits for them, and re-layouts  40.2 us (4%)
  between operations  15.3 us (2%)
    reduce_scatter x2, waiting for transfers between devices, per_device(): forward = lax.psum_scatter(row_part, 'col', scatter_dimension=0, tiled=True)  146 us
    dot_general x16, matrix products, place_sum(): jnp.einsum('gt,giv->tiv', table, upper, preferred_element_type=jnp.float32)  145 us
    reduce_scatter x2, waiting for transfers between devices, per_device(): lax.psum_scatter(col_part, 'row', scatter_dimension=0, tiled=True)  143 us
    all_gather x2, waiting for transfers between devices, per_device(): cols_side = lax.all_gather(operand, 'row', axis=0, tiled=True)  115 us
    dot_general x8, matrix products, group_step(): jnp.einsum('gji,gjv->giv', block_tile, row_picked, preferred_element_type...  105 us
    dot_general x16, matrix products, place_sum(): jnp.einsum('gt,giv->tiv', table, lower, preferred_element_type=jnp.float32)  83.7 us
    all_gather x2, waiting for transfers between devices, per_device(): rows_side = lax.all_gather(operand, 'col', axis=0, tiled=True)  75.1 us
    dot_general x8, matrix products, group_step(): jnp.einsum('gij,gjv->giv', block_tile, col_picked, preferred_element_type...  63.9 us
  transfers between devices with their start and end apart: 8, of which 8 were waited for; matrix products, arithmetic and copies ran while one was open for 2% of the time, Pallas kernels for 0%

commit v1 on v0

v1 whole, which is shorter than its diff:
```python
import functools

import jax
import jax.numpy as jnp
from jax import lax
from jax.experimental import pallas as pl
from jax.experimental.pallas import tpu as pltpu
from jax.sharding import PartitionSpec as P

DEGREE = 2
UNROLL = 4


def slot_kernel(
    rows_ref, cols_ref, count_ref, blocks_ref, row_side, col_side, row_out, col_out, row_acc, col_acc
):
    group = pl.program_id(0)
    group_size = blocks_ref.shape[0]

    @pl.when(group == 0)
    def _():
        row_acc[...] = jnp.zeros_like(row_acc)
        col_acc[...] = jnp.zeros_like(col_acc)

    first = group * group_size
    live = jnp.clip(count_ref[0] - first, 0, group_size)

    def one_slot(k):
        row = rows_ref[first + k]
        col = cols_ref[first + k]
        block = blocks_ref[k]
        forward = jnp.dot(block, col_side[col], preferred_element_type=jnp.float32)
        mirror = lax.dot_general(
            block, row_side[row], (((0,), (0,)), ((), ())), preferred_element_type=jnp.float32
        )
        return row, col, forward, mirror

    def add(found):
        row, col, forward, mirror = found
        row_acc[row] += forward
        col_acc[col] += mirror

    def step(i, carry):
        found = [one_slot(i * UNROLL + u) for u in range(UNROLL)]
        for f in found:
            add(f)
        return carry

    whole = live // UNROLL
    lax.fori_loop(0, whole, step, 0)

    def rest(k, carry):
        add(one_slot(k))
        return carry

    lax.fori_loop(whole * UNROLL, live, rest, 0)

    @pl.when(group == pl.num_programs(0) - 1)
    def _():
        row_out[...] = row_acc[...].astype(row_out.dtype)
        col_out[...] = col_acc[...].astype(col_out.dtype)


def slot_products(local_blocks, local_rows, local_cols, slot_count, rows_side, cols_side):
    slots, order, _ = local_blocks.shape
    width = rows_side.shape[1]
    row_tiles = rows_side.reshape(-1, order, width)
    col_tiles = cols_side.reshape(-1, order, width)
    group_size = min(32, slots)

    def block_map(g, rows, cols, count):
        last = jnp.maximum((count[0] + group_size - 1) // group_size - 1, 0)
        return (jnp.minimum(g, last), 0, 0)

    def whole(g, rows, cols, count):
        return (0, 0, 0)

    row_part, col_part = pl.pallas_call(
        slot_kernel,
        grid_spec=pltpu.PrefetchScalarGridSpec(
            num_scalar_prefetch=3,
            grid=(slots // group_size,),
            in_specs=[
                pl.BlockSpec((group_size, order, order), block_map),
                pl.BlockSpec(row_tiles.shape, whole, pipeline_mode=pl.Buffered(1)),
                pl.BlockSpec(col_tiles.shape, whole, pipeline_mode=pl.Buffered(1)),
            ],
            out_specs=[
                pl.BlockSpec(row_tiles.shape, whole, pipeline_mode=pl.Buffered(1)),
                pl.BlockSpec(col_tiles.shape, whole, pipeline_mode=pl.Buffered(1)),
            ],
            scratch_shapes=[
                pltpu.VMEM(row_tiles.shape, jnp.float32),
                pltpu.VMEM(col_tiles.shape, jnp.float32),
            ],
        ),
        out_shape=[
            jax.ShapeDtypeStruct(row_tiles.shape, jnp.bfloat16),
            jax.ShapeDtypeStruct(col_tiles.shape, jnp.bfloat16),
        ],
        compiler_params=pltpu.CompilerParams(vmem_limit_bytes=44 * 1024 * 1024),
        cost_estimate=pl.CostEstimate(
            flops=4 * slots * order * order * width, bytes_accessed=20 * 1024 * 1024, transcendentals=0
        ),
    )(local_rows, local_cols, slot_count, local_blocks, row_tiles, col_tiles)
    return row_part.reshape(-1, width), col_part.reshape(-1, width)


def split_sum(part, axis, members):
    pieces = lax.all_to_all(part, axis, 0, 0, tiled=True)
    pieces = pieces.reshape(members, -1, part.shape[1])
    return jnp.sum(pieces.astype(jnp.float32), axis=0)


def per_device(
    vectors, blocks, block_rows, block_cols, block_count, lower_edge, upper_edge, *, row_size, col_size
):
    center = (upper_edge[0] + lower_edge[0]) * 0.5
    half_width = (upper_edge[0] - lower_edge[0]) * 0.5
    local_blocks = blocks[0, 0]
    local_rows = block_rows[0, 0]
    local_cols = block_cols[0, 0]
    slot_count = block_count[0]
    current = vectors.astype(jnp.float32)
    previous = jnp.zeros_like(current)
    for degree in range(DEGREE):
        operand = current.astype(jnp.bfloat16)
        cols_side = lax.all_gather(operand, "row", axis=0, tiled=True)
        rows_side = lax.all_gather(operand, "col", axis=0, tiled=True)
        row_part, col_part = slot_products(
            local_blocks, local_rows, local_cols, slot_count, rows_side, cols_side
        )
        applied = split_sum(row_part, "col", col_size) + split_sum(col_part, "row", row_size)
        shifted = applied - center * current
        if degree == 0:
            following = shifted / half_width
        else:
            following = 2.0 * shifted / half_width - previous
        previous, current = (current, following)
    return current


def solution(mesh):
    sizes = dict(mesh.shape)
    return jax.shard_map(
        functools.partial(per_device, row_size=sizes["row"], col_size=sizes["col"]),
        mesh=mesh,
        in_specs=(
            P(("row", "col"), None),
            P("row", "col", None, None, None),
            P("row", "col", None),
            P("row", "col", None),
            P("row", "col"),
            P(),
            P(),
        ),
        out_specs=P(("row", "col"), None),
        check_vma=False,
    )
```

time: 1010 us -> 430 us (0.43); the launches traced: 995 us -> 430 us
  matrix products: 448 us -> 0 us
  waiting for transfers between devices: 480 us -> 294 us
  blocking collectives: 0 us -> 75.3 us
  local copies, waits for them, and re-layouts: 40.2 us -> 4.57 us
  Pallas kernels: 0 us -> 20.8 us
  starting transfers between devices: 0.29 us -> 10.4 us
    dot_general x64 -> x0, matrix products: 448 us -> none  [the longest x16 145 us: place_sum(): jnp.einsum('gt,giv->tiv', table, upper, preferred_element_type=jnp.float32)]
    reduce_scatter x4 -> x0, waiting for transfers between devices: 288 us -> none  [the longest x2 146 us: per_device(): forward = lax.psum_scatter(row_part, 'col', scatter_dimension=0, tiled=True)]
    all_to_all x0 -> x2, waiting for transfers between devices: none -> 109 us  [split_sum(): pieces = lax.all_to_all(part, axis, 0, 0, tiled=True)]
    all_to_all x0 -> x2, blocking collectives: none -> 75.3 us  [split_sum(): pieces = lax.all_to_all(part, axis, 0, 0, tiled=True)]
    while x60 -> x0, local copies, waits for them, and re-layouts: 36.2 us -> none  [the longest x4 36.1 us: slot_products(): lax.fori_loop(0, group_limit, group_step, start_totals)]
    pallas_call x0 -> x2, Pallas kernels: none -> 20.8 us  [slot_products(): pl.pallas_call(slot_kernel, grid_spec=pltpu.PrefetchScalarGridSpec(num_sc...]
    all_to_all x0 -> x2, starting transfers between devices: none -> 10.3 us  [split_sum(): pieces = lax.all_to_all(part, axis, 0, 0, tiled=True)]
  transfers between devices with their start and end apart: 8 -> 6, of which waited for: 8 -> 6; matrix products, arithmetic and copies ran while one was open for 2% -> 0% of each run, Pallas kernels for 0% -> 0%
where the time goes in v1:
time: 430 us
  waiting for transfers between devices  294 us (68%)
  blocking collectives  75.3 us (18%)
  Pallas kernels  20.8 us (5%)
  between operations  15.2 us (4%)
  starting transfers between devices  10.4 us (2%)
  other arithmetic  8.87 us (2%)
  local copies, waits for them, and re-layouts  4.57 us (1%)
    all_to_all x2, waiting for transfers between devices, split_sum(): pieces = lax.all_to_all(part, axis, 0, 0, tiled=True)  109 us
    all_gather x2, waiting for transfers between devices, per_device(): cols_side = lax.all_gather(operand, 'row', axis=0, tiled=True)  109 us
    all_to_all x2, blocking collectives, split_sum(): pieces = lax.all_to_all(part, axis, 0, 0, tiled=True)  75.3 us
    all_gather x2, waiting for transfers between devices, per_device(): rows_side = lax.all_gather(operand, 'col', axis=0, tiled=True)  75 us
    pallas_call x2, Pallas kernels, slot_products(): pl.pallas_call(slot_kernel, grid_spec=pltpu.PrefetchScalarGridSpec(num_sc...  20.8 us
    all_to_all x2, starting transfers between devices, split_sum(): pieces = lax.all_to_all(part, axis, 0, 0, tiled=True)  10.3 us
  transfers between devices with their start and end apart: 6, of which 6 were waited for; matrix products, arithmetic and copies ran while one was open for 0% of the time, Pallas kernels for 0%

profile of v1, /device:TPU:1, one launch (start us, length us, event | category | flops | bytes accessed | tf_op | source)
XLA Modules:
  0.0 429.6 jit_solution(1616470794035820409)
XLA Ops:
  6.5 0.0 all-gather.7.cloned.1.call-start
  6.5 0.7 all-gather.7.cloned.1.call-update
  7.3 0.0 all-gather.5.cloned.1.call-start
  7.3 0.7 all-gather.5.cloned.1.call-update
  8.7 58.1 %all-gather.7.cloned.1.call-done = bf16[4096,256]{1,0:T(8,128)(2,1)} async-done(((bf16[512,256]{1,0:T(8,128)(2,1)}), bf16[4096,256]{1,0:T(8,128)(2,1)}) %all-gather.7.cloned.1.call-update) | async-done | bytes 2097168 | tf_op jit(solution)/shard_map/all_gather | solution.py:128
  66.7 37.6 %all-gather.5.cloned.1.call-done = bf16[8192,256]{1,0:T(8,128)(2,1)} async-done(((bf16[512,256]{1,0:T(8,128)(2,1)}), bf16[8192,256]{1,0:T(8,128)(2,1)}) %all-gather.5.cloned.1.call-update) | async-done | bytes 4194320 | tf_op jit(solution)/shard_map/all_gather | solution.py:129
  104.3 0.0 copy-start.3
  104.3 1.6 copy-done.3
  105.9 0.0 copy-start.4
  105.9 0.7 copy-done.4
  106.6 0.0 copy-start.6
  106.6 0.7 copy-done.6
  107.2 10.4 %shard_map.73 = (bf16[64,128,256]{2,1,0:T(8,128)(2,1)S(1)}, bf16[32,128,256]{2,1,0:T(8,128)(2,1)S(1)}) custom-call(s32[256]{0:T(256)S(1)} %bitcast.22, s32[256]{0:T(256)S(1)} %bitcast.24, s32[1]{0:T(128)} %bitcast.14.count_ref, bf16[256,128,128]{2,1,0:T(8,128)(2,1)} %bitcast.26, bf16[64,128,256]{2,1,0:T(8,128)(2,1)} %bitcast.29, ...), custom_call_target="tpu_custom_call" | custom-call | flops 4294967296 | bytes 20971520 | tf_op jit(solution)/shard_map/pallas_call | solution.py:78
  117.7 0.0 copy-start
  117.7 37.6 %all_to_all.36 = bf16[8,512,256]{2,1,0:T(8,128)(2,1)S(1)} all-to-all(bf16[8,512,256]{2,1,0:T(8,128)(2,1)S(1)} %bitcast.19), channel_id=1, replica_groups=mesh['row'=8,'col'=16] {'row'}, dimensions={0} | all-to-all | bytes 4194304 | tf_op jit(solution)/shard_map/all_to_all | solution.py:110
  155.3 0.0 copy-done
  155.3 5.2 %all-to-all-start = ((bf16[16,512,256]{2,1,0:T(8,128)(2,1)}), bf16[16,512,256]{2,1,0:T(8,128)(2,1)}, u32[]{:S(2)}, u32[]{:S(2)}) async-start(bf16[16,512,256]{2,1,0:T(8,128)(2,1)} %bitcast.16), calls=%async_computation | async-start | bytes 8388608 | tf_op jit(solution)/shard_map/all_to_all | solution.py:110
  160.5 0.0 copy-start.8
  160.5 0.0 all-gather.11.cloned.1.call-start
  161.8 0.0 copy-start.5
  161.9 0.0 copy-start.7
  161.9 0.3 convert_reduce_fusion.3
  162.2 54.1 %all-to-all-done = bf16[16,512,256]{2,1,0:T(8,128)(2,1)} async-done(((bf16[16,512,256]{2,1,0:T(8,128)(2,1)}), bf16[16,512,256]{2,1,0:T(8,128)(2,1)}, u32[]{:S(2)}, u32[]{:S(2)}) %all-to-all-start) | async-done | bytes 4194336 | tf_op jit(solution)/shard_map/all_to_all | solution.py:110
  216.3 2.8 convert_reduce_fusion.1
  219.1 0.0 copy-done.8
  219.1 0.8 fusion.2
  219.9 0.0 all-gather.11.cloned.1.call-update
  219.9 0.0 all-gather.9.cloned.1.call-start
  220.0 0.5 all-gather.9.cloned.1.call-update
  220.5 50.7 %all-gather.11.cloned.1.call-done = bf16[4096,256]{1,0:T(8,128)(2,1)} async-done(((bf16[512,256]{1,0:T(8,128)(2,1)}), bf16[4096,256]{1,0:T(8,128)(2,1)}) %all-gather.11.cloned.1.call-update) | async-done | bytes 2097168 | tf_op jit(solution)/shard_map/all_gather | solution.py:128
  271.2 37.4 %all-gather.9.cloned.1.call-done = bf16[8192,256]{1,0:T(8,128)(2,1)} async-done(((bf16[512,256]{1,0:T(8,128)(2,1)}), bf16[8192,256]{1,0:T(8,128)(2,1)}) %all-gather.9.cloned.1.call-update) | async-done | bytes 4194320 | tf_op jit(solution)/shard_map/all_gather | solution.py:129
  308.6 0.0 copy-done.5
  308.6 0.0 copy-done.7
  308.6 0.0 copy-start.2
  308.6 1.6 copy-done.2
  310.2 10.4 %shard_map.74 = (bf16[64,128,256]{2,1,0:T(8,128)(2,1)S(1)}, bf16[32,128,256]{2,1,0:T(8,128)(2,1)S(1)}) custom-call(s32[256]{0:T(256)S(1)} %bitcast.23, s32[256]{0:T(256)S(1)} %bitcast.25, s32[1]{0:T(128)} %bitcast.15.count_ref, bf16[256,128,128]{2,1,0:T(8,128)(2,1)} %bitcast.27, bf16[64,128,256]{2,1,0:T(8,128)(2,1)} %bitcast.28, ...), custom_call_target="tpu_custom_call" | custom-call | flops 4294967296 | bytes 20971520 | tf_op jit(solution)/shard_map/pallas_call | solution.py:78
  320.6 0.0 copy-start.1
  320.6 37.6 %all_to_all.37 = bf16[8,512,256]{2,1,0:T(8,128)(2,1)S(1)} all-to-all(bf16[8,512,256]{2,1,0:T(8,128)(2,1)S(1)} %bitcast.18), channel_id=1, replica_groups=mesh['row'=8,'col'=16] {'row'}, dimensions={0} | all-to-all | bytes 4194304 | tf_op jit(solution)/shard_map/all_to_all | solution.py:110
  358.3 0.0 copy-done.1
  358.3 5.1 %all-to-all-start.2 = ((bf16[16,512,256]{2,1,0:T(8,128)(2,1)}), bf16[16,512,256]{2,1,0:T(8,128)(2,1)}, u32[]{:S(2)}, u32[]{:S(2)}) async-start(bf16[16,512,256]{2,1,0:T(8,128)(2,1)} %bitcast.17), calls=%async_computation.2 | async-start | bytes 8388608 | tf_op jit(solution)/shard_map/all_to_all | solution.py:110
  363.4 1.1 convert_reduce_fusion.2
  364.5 0.0 copy-start.9
  364.5 54.7 %all-to-all-done.2 = bf16[16,512,256]{2,1,0:T(8,128)(2,1)} async-done(((bf16[16,512,256]{2,1,0:T(8,128)(2,1)}), bf16[16,512,256]{2,1,0:T(8,128)(2,1)}, u32[]{:S(2)}, u32[]{:S(2)}) %all-to-all-start.2) | async-done | bytes 4194336 | tf_op jit(solution)/shard_map/all_to_all | solution.py:110
  419.2 2.8 convert_reduce_fusion
  422.0 0.0 copy-done.9
  422.0 1.1 convert_subtract_fusion
Async XLA Ops:
  6.5 60.2 %all-gather.7.cloned.1.call-start = ((), (), s32[]{:S(2)}) async-start(), calls=%async_computation.5 | async-start | bytes 2359296 | tf_op jit(solution)/shard_map/all_gather | solution.py:128
  7.3 97.0 %all-gather.5.cloned.1.call-start = ((), (), s32[]{:S(2)}) async-start(), calls=%async_computation.4 | async-start | bytes 4456448 | tf_op jit(solution)/shard_map/all_gather | solution.py:129
  104.3 1.6 copy-start.3
  105.9 0.7 copy-start.4
  106.6 0.7 copy-start.6
  117.7 37.6 %copy-start = (bf16[64,128,256]{2,1,0:T(8,128)(2,1)}, bf16[64,128,256]{2,1,0:T(8,128)(2,1)S(1)}, u32[]{:S(2)}) copy-start(bf16[64,128,256]{2,1,0:T(8,128)(2,1)S(1)} %get-tuple-element.9) | copy-start | bytes 12582916
  155.3 61.0 %all-to-all-start = ((bf16[16,512,256]{2,1,0:T(8,128)(2,1)}), bf16[16,512,256]{2,1,0:T(8,128)(2,1)}, u32[]{:S(2)}, u32[]{:S(2)}) async-start(bf16[16,512,256]{2,1,0:T(8,128)(2,1)} %bitcast.16), calls=%async_computation | async-start | bytes 8388608 | tf_op jit(solution)/shard_map/all_to_all | solution.py:110
  160.5 58.6 %copy-start.8 = (bf16[512,256]{1,0:T(8,128)(2,1)S(1)}, bf16[512,256]{1,0:T(8,128)(2,1)}, u32[]{:S(2)}) copy-start(bf16[512,256]{1,0:T(8,128)(2,1)} %param.7) | copy-start | bytes 786436
  160.5 110.7 %all-gather.11.cloned.1.call-start = ((), (), s32[]{:S(2)}) async-start(), calls=%async_computation.7 | async-start | bytes 2359296 | tf_op jit(solution)/shard_map/all_gather | solution.py:128
  161.8 146.8 %copy-start.5 = (s32[1,1,256]{2,1,0:T(1,128)S(1)}, s32[1,1,256]{2,1,0:T(1,128)}, u32[]{:S(2)}) copy-start(s32[1,1,256]{2,1,0:T(1,128)} %param.9) | copy-start | bytes 3076
  161.9 146.7 %copy-start.7 = (s32[1,1,256]{2,1,0:T(1,128)S(1)}, s32[1,1,256]{2,1,0:T(1,128)}, u32[]{:S(2)}) copy-start(s32[1,1,256]{2,1,0:T(1,128)} %param.10) | copy-start | bytes 3076
  219.9 88.7 %all-gather.9.cloned.1.call-start = ((), (), s32[]{:S(2)}) async-start(), calls=%async_computation.6 | async-start | bytes 4456448 | tf_op jit(solution)/shard_map/all_gather | solution.py:129
  308.6 1.6 copy-start.2
  320.6 37.6 %copy-start.1 = (bf16[64,128,256]{2,1,0:T(8,128)(2,1)}, bf16[64,128,256]{2,1,0:T(8,128)(2,1)S(1)}, u32[]{:S(2)}) copy-start(bf16[64,128,256]{2,1,0:T(8,128)(2,1)S(1)} %get-tuple-element.11) | copy-start | bytes 12582916
  358.3 61.0 %all-to-all-start.2 = ((bf16[16,512,256]{2,1,0:T(8,128)(2,1)}), bf16[16,512,256]{2,1,0:T(8,128)(2,1)}, u32[]{:S(2)}, u32[]{:S(2)}) async-start(bf16[16,512,256]{2,1,0:T(8,128)(2,1)} %bitcast.17), calls=%async_computation.2 | async-start | bytes 8388608 | tf_op jit(solution)/shard_map/all_to_all | solution.py:110
  364.5 57.5 %copy-start.9 = (f32[512,256]{1,0:T(8,128)S(1)}, f32[512,256]{1,0:T(8,128)}, u32[]{:S(2)}) copy-start(f32[512,256]{1,0:T(8,128)} %convert_reduce_fusion.2) | copy-start | bytes 1572868
Sparse Core Ops, SparseCore 0:
  9.7 56.9 all-gather.6
  68.4 35.8 all-gather.4
  220.0 51.0 all-gather.10
  272.7 35.8 all-gather.8
